TPU v7x, 32 devices: a whole 2x2x4 slice. The times are simulated.
32 devices in a mesh: groups: 2 (over y), freq: 8 (over z, core), mat: 2 (over x).
Axes of the slice: x: 2, y: 2, z: 4, core: 2. Of those that a mesh axis runs over, the one named last changes fastest.
Arguments:
- traces: bfloat16 [32, 2048, 512], P(('groups', 'freq'), 'mat'), parts along dimension 0, may hold values from -6 to 6
- point_index: int32 [32, 2, 1024], P(('groups', 'freq'), 'mat'), parts along dimension 0, may hold values from 0 to 1023, each once within a row
- spectral_slot_number: int32 [16], P('groups'), parts along dimension 0, may hold values from 1 to 255
Outputs:
- multiples: float32 [32, 8, 2, 16], P(('groups', 'mat'), 'freq'), parts along dimension 0
There are 2 independent parts, one for each index of `groups`. A program takes and returns all parts, laid end to end along the dimension named above; each array names one. Nothing has to cross between parts.
All inputs are finite; a program needn't handle non-finite values.
Results may differ from a plain program's by a relative error of at most 0.0059.
Values may be sent and summed in bfloat16 or wider, within the bound.
A program may use at most 64 MiB of HBM per device.

v0:
```python
import math

import jax
import jax.numpy as jnp
from jax import lax
from jax.sharding import PartitionSpec as P

PATCH_POINTS = 2048


def fourier_table(spectral_slot_number, record_duration):
    clock_moments = jnp.arange(record_duration, dtype=jnp.int32)
    angular_steps_list = spectral_slot_number[:, None] * clock_moments[None, :] % record_duration
    phases = 2.0 * math.pi / record_duration * angular_steps_list.astype(jnp.float32)
    edge_damping_coefficients = 0.5 - 0.5 * jnp.cos(
        2.0 * math.pi / record_duration * (clock_moments.astype(jnp.float32) + 0.5)
    )
    weighting = edge_damping_coefficients / math.sqrt(record_duration)
    stacked = jnp.stack([jnp.cos(phases) * weighting, -jnp.sin(phases) * weighting], axis=1)
    return stacked.reshape(2 * spectral_slot_number.shape[0], record_duration).astype(jnp.bfloat16)


def contract(left_rows, right_rows):
    freq_local, parts, row_count, width = left_rows.shape
    column_count = right_rows.shape[2]
    left_flat = left_rows.reshape(freq_local, parts * row_count, width)
    right_flat = right_rows.reshape(freq_local, parts * column_count, width)
    joined = lax.dot_general(
        left_flat, right_flat, (((2,), (2,)), ((0,), (0,))), preferred_element_type=jnp.float32
    )
    joined = joined.reshape(freq_local, parts, row_count, parts, column_count)
    output_real = joined[:, 0, :, 0] - joined[:, 1, :, 1]
    imag_out = joined[:, 0, :, 1] + joined[:, 1, :, 0]
    return jnp.stack([output_real, imag_out], axis=1)


def reorder_rows(rows, order):
    return rows[order]


def local(traces, point_index, spectral_slot_number):
    shot_local, block_span_size, record_duration = traces.shape
    fourier = fourier_table(spectral_slot_number, record_duration)
    arrangement = point_index.reshape(shot_local, block_span_size)
    ordered = jax.vmap(reorder_rows)(traces, arrangement)
    spectra = jnp.einsum("jt,spt->jsp", fourier, ordered, preferred_element_type=jnp.float32)
    spectra = spectra.astype(jnp.bfloat16)
    freq_count = lax.axis_size("freq")
    freq_local = spectra.shape[0] // (2 * freq_count)
    spectra = spectra.reshape(freq_count, 2 * freq_local, shot_local, block_span_size)
    owned = lax.all_to_all(spectra, "freq", split_axis=0, concat_axis=2, tiled=True)
    shot_count = owned.shape[2]
    panel_count = lax.axis_size("mat")
    number_of_lines = shot_count // panel_count
    factor = 4.0 / math.sqrt(PATCH_POINTS)
    first_row = lax.axis_index("mat") * number_of_lines
    panel = lax.all_gather(owned, "mat", axis=3, tiled=True)
    own_rows = lax.dynamic_slice_in_dim(panel, first_row, number_of_lines, 2)
    running = contract(own_rows, panel)
    return jnp.transpose(running * factor, (2, 0, 1, 3))


def solution(mesh):
    placed = (P(("groups", "freq"), "mat", None), P(("groups", "freq"), "mat", None), P("groups"))
    return jax.shard_map(
        local,
        mesh=mesh,
        in_specs=placed,
        out_specs=P(("groups", "mat"), "freq", None, None),
        check_vma=False,
    )
```

profile of v0, /device:TPU:0, one launch (start us, length us, event | category | flops | bytes accessed | tf_op | source)
XLA Modules:
  0.0 46.9 jit_solution(2093953662919186985)
XLA Ops:
  0.0 0.0 copy-start
  0.1 1.0 %multiply_convert_fusion.1 = (bf16[8,1,512]{2,0,1:T(8,128)(2,1)S(1)}, bf16[8,1,512]{2,0,1:T(8,128)(2,1)S(1)}) fusion(f32[512]{0:T(512)S(1)} %subtract_multiply_fusion, s32[8]{0:T(128)} %param.5), kind=kLoop, calls=%fused_computation.15 | loop fusion | flops 77824 | bytes 18464 | tf_op jit(solution)/shard_map/convert
  1.1 0.7 %fusion.11 = s32[2,1024,1]{1,2,0:T(1,128)S(1)} fusion(s32[2,1,1024]{2,1,0:T(1,128)} %param.4), kind=kLoop, calls=%fused_computation.21 | loop fusion | flops 16384 | bytes 16384 | tf_op jit(solution)/shard_map/vmap()/gather | solution.py:38
  1.8 0.0 copy-done
  1.8 24.0 %gather_fusion = bf16[2048,512]{1,0:T(8,128)(2,1)} fusion(bf16[2,1024,512]{2,1,0:T(8,128)(2,1)S(1)} %copy-done, s32[2048]{0:T(1024)S(1)} %bitcast.31), kind=kCustom, calls=%fused_computation | custom fusion | bytes 4210688 | tf_op jit(solution)/shard_map/vmap()/gather | solution.py:38
  25.8 2.2 %convolution_convert_fusion = bf16[16,2,1024]{2,0,1:T(8,128)(2,1)S(1)} fusion(bf16[16,512,1]{1,0,2:T(8,128)(2,1)S(1)} %reshape.304, bf16[2,1024,512]{2,1,0:T(8,128)(2,1)} %bitcast.32), kind=kOutput, calls=%fused_computation.1 | convolution fusion | flops 33587200 | bytes 2179072 | tf_op jit(solution)/shard_map/jt,spt->jsp/dot_general | solution.py:46
  28.1 0.7 %copy.13 = bf16[8,2,2,1024]{3,1,2,0:T(2,128)(2,1)} copy(bf16[8,2,2,1024]{3,1,0,2:T(2,128)(2,1)S(1)} %reshape.296) | data formatting | bytes 131072 | tf_op jit(solution)/shard_map/reshape | solution.py:50
  28.8 6.3 %all-to-all-start = ((bf16[8,2,2,1024]{3,1,2,0:T(2,128)(2,1)}), bf16[8,2,2,1024]{3,1,2,0:T(2,128)(2,1)S(1)}, u32[]{:S(2)}, u32[]{:S(2)}) async-start(bf16[8,2,2,1024]{3,1,2,0:T(2,128)(2,1)} %copy.13), calls=%async_computation | async-start | bytes 131072 | tf_op jit(solution)/shard_map/all_to_all | solution.py:51
  35.1 5.9 %all-to-all-done = bf16[8,2,2,1024]{3,1,2,0:T(2,128)(2,1)S(1)} async-done(((bf16[8,2,2,1024]{3,1,2,0:T(2,128)(2,1)}), bf16[8,2,2,1024]{3,1,2,0:T(2,128)(2,1)S(1)}, u32[]{:S(2)}, u32[]{:S(2)}) %all-to-all-start) | async-done | bytes 65568 | tf_op jit(solution)/shard_map/all_to_all | solution.py:51
  41.0 4.9 %all_gather.3 = bf16[1,2,16,2048]{3,2,1,0:T(8,128)(2,1)S(1)} all-gather(bf16[1,2,16,1024]{3,2,1,0:T(8,128)(2,1)S(1)} %copy.17), channel_id=1, replica_groups=mesh['groups'=2,'freq'=8,'mat'=2] {'mat'}, dimensions={3}, use_global_device_ids=true | all-gather | bytes 196608 | tf_op jit(solution)/shard_map/all_gather | solution.py:57
  46.0 0.3 convolution_bitcast_fusion
  46.3 0.6 %copy.15 = f32[8,1,2,16]{3,2,1,0:T(2,128)} copy(f32[8,1,2,16]{3,0,2,1:T(8,128)S(1)} %fusion.12) | data formatting | bytes 2048 | tf_op jit(solution)/shard_map/transpose | solution.py:60
  (8 shorter events, 0.2 us)
Async XLA Ops:
  0.0 1.8 %copy-start = (bf16[2,1024,512]{2,1,0:T(8,128)(2,1)S(1)}, bf16[2,1024,512]{2,1,0:T(8,128)(2,1)}, u32[]{:S(2)}) copy-start(bf16[2,1024,512]{2,1,0:T(8,128)(2,1)} %param.3) | copy-start | bytes 6291460
  28.8 12.2 %all-to-all-start = ((bf16[8,2,2,1024]{3,1,2,0:T(2,128)(2,1)}), bf16[8,2,2,1024]{3,1,2,0:T(2,128)(2,1)S(1)}, u32[]{:S(2)}, u32[]{:S(2)}) async-start(bf16[8,2,2,1024]{3,1,2,0:T(2,128)(2,1)} %copy.13), calls=%async_computation | async-start | bytes 131072 | tf_op jit(solution)/shard_map/all_to_all | solution.py:51
where the time goes:
time: 47.2 us; the launch traced here: 46.9 us
  local copies, waits for them, and re-layouts  25.4 us (54%)
  starting transfers between devices  6.33 us (13%)
  waiting for transfers between devices  5.92 us (13%)
  blocking collectives  4.94 us (10%)
  matrix products  2.49 us (5%)
  other arithmetic  1.74 us (4%)
    gather x1, local copies, waits for them, and re-layouts, reorder_rows(): return rows[order]  24 us
    all_to_all x1, starting transfers between devices, local(): lax.all_to_all(spectra, 'freq', split_axis=0, concat_axis=2, tiled=True)  6.33 us
    all_to_all x1, waiting for transfers between devices, local(): lax.all_to_all(spectra, 'freq', split_axis=0, concat_axis=2, tiled=True)  5.92 us
    all_gather x1, blocking collectives, local(): panel = lax.all_gather(owned, 'mat', axis=3, tiled=True)  4.94 us
    dot_general x1, matrix products, local(): jnp.einsum('jt,spt->jsp', fourier, ordered, preferred_element_type=jnp.fl...  2.23 us
    another operation x1, other arithmetic  0.95 us
  transfers between devices with their start and end apart: 1, of which 1 were waited for; matrix products, arithmetic and copies ran while one was open for 0% of the time, Pallas kernels for 0%

commit v1 on v0

v1 whole, which is shorter than its diff:
```python
import functools
import math

import jax
import jax.numpy as jnp
from jax import lax
from jax.experimental import pallas as pl
from jax.experimental.pallas import tpu as pltpu
from jax.sharding import PartitionSpec as P

MESH = pl.DeviceIdType.MESH
LANES = 128
SUB = 8


def sine(x):
    y = x * x
    total = jnp.full_like(y, -1.0 / math.factorial(11))
    for order in (9, 7, 5, 3, 1):
        total = total * y + (-1.0) ** (order // 2) / math.factorial(order)
    return total * x


def cosine_of(turns, period):
    return sine((jnp.abs(turns - 0.5 * period) - 0.25 * period) * (2.0 * math.pi / period))


def kernel(nf, nm, factor, traces_hbm, index_hbm, slots_hbm, out_ref,
           slots, index, traces, table, send, recv, wide, part, land,
           slot_sem, index_sem, trace_sem, send_sem, recv_sem, part_send_sem, part_recv_sem):
    shots, points, moments = traces.shape
    chunks = points // LANES
    halves = trace_sem.shape[1]
    span = points // halves
    me, column = lax.axis_index("freq"), lax.axis_index("mat")

    slot_copy = pltpu.make_async_copy(slots_hbm, slots, slot_sem)
    slot_copy.start()
    trace_copies = []
    for s in range(shots):
        trace_copies.append([])
        for h in range(halves):
            rows = pl.ds(h * span, span)
            copy = pltpu.make_async_copy(traces_hbm.at[s, rows], traces.at[s, rows], trace_sem.at[s, h])
            copy.start()
            trace_copies[s].append(copy)
        if s == 0:
            index_copy = pltpu.make_async_copy(index_hbm, index, index_sem)
            index_copy.start()

    barrier = pltpu.get_barrier_semaphore()
    for k in range(1, nf):
        pl.semaphore_signal(barrier, inc=1, device_id={"freq": lax.rem(me + k, nf)}, device_id_type=MESH)
    for k in range(1, nm):
        pl.semaphore_signal(barrier, inc=1, device_id={"mat": lax.rem(column + k, nm)}, device_id_type=MESH)

    moment = lax.broadcasted_iota(jnp.int32, (SUB, moments), 1)
    taper = 0.5 - 0.5 * cosine_of(moment.astype(jnp.float32) + 0.5, moments)
    weight = taper * (1.0 / math.sqrt(moments))
    row = lax.broadcasted_iota(jnp.int32, (SUB, moments), 0)
    slot_copy.wait()
    for base in range(0, nf, SUB):
        number = jnp.zeros((SUB, moments), jnp.int32)
        for k in range(base, min(base + SUB, nf)):
            number = jnp.where(row == k - base, slots[lax.rem(me + k, nf)], number)
        steps = (number * moment) & (moments - 1)
        quarter = (steps + moments // 4) & (moments - 1)
        pair = [cosine_of(m.astype(jnp.float32), moments) * weight for m in (steps, quarter)]
        for k in range(base, min(base + SUB, nf)):
            both = [jnp.broadcast_to(p[k - base:k - base + 1], (SUB, moments)) for p in pair]
            table[2 * SUB * k:2 * SUB * (k + 1), :] = jnp.concatenate(both, 0).astype(jnp.bfloat16)

    part[...] = jnp.zeros_like(part)
    index_copy.wait()
    copies = {}
    for s in range(shots):
        raw = []
        for h in range(halves):
            trace_copies[s][h].wait()
            raw.append(lax.dot_general(
                table[...], traces[s, h * span:(h + 1) * span, :], (((1,), (1,)), ((), ())),
                preferred_element_type=jnp.float32))
        raw = jnp.concatenate(raw, 1) if halves > 1 else raw[0]
        place = index[s]
        if chunks < SUB:
            place = jnp.concatenate([place] * (SUB // chunks), 0)
        low, high = place & (LANES - 1), place // LANES
        if s == 0:
            pl.semaphore_wait(barrier, nf - 1 + nm - 1)
        for k in list(range(1, nf)) + [0]:
            both = []
            for c in range(2):
                first = (2 * k + c) * SUB
                got = None
                for j in range(chunks):
                    piece = raw[first:first + SUB, j * LANES:(j + 1) * LANES]
                    piece = jnp.take_along_axis(piece, low, axis=1)
                    got = piece if j == 0 else jnp.where(high == j, piece, got)
                both.append(got)
            both = jnp.concatenate(both, 0)
            if k == 0:
                first = pl.multiple_of((me * shots + s) * 2 * SUB, 2 * SUB)
                wide[pl.ds(first, 2 * SUB), :] = both.astype(jnp.bfloat16).astype(jnp.float32)
                continue
            send[s, k] = both.astype(jnp.bfloat16)
            copies[s, k] = pltpu.make_async_remote_copy(
                src_ref=send.at[s, k], dst_ref=recv.at[s, k],
                send_sem=send_sem.at[s, k], recv_sem=recv_sem.at[s, k],
                device_id={"freq": lax.rem(me + k, nf)}, device_id_type=MESH)
            copies[s, k].start()

    for s in range(shots):
        for k in range(1, nf):
            copies[s, k].wait_recv()
            source = lax.rem(me + nf - k, nf)
            first = pl.multiple_of((source * shots + s) * 2 * SUB, 2 * SUB)
            wide[pl.ds(first, 2 * SUB), :] = recv[s, k].astype(jnp.float32)

    count = nf * shots
    real, imag = [
        jnp.concatenate([wide[pl.ds(c * SUB + j, count, stride=2 * SUB), :] for j in range(chunks)], 1)
        for c in range(2)]
    left = jnp.concatenate([real, imag], 1).astype(jnp.bfloat16)
    right = jnp.concatenate(
        [jnp.concatenate([real, -imag], 1), jnp.concatenate([imag, real], 1)], 0).astype(jnp.bfloat16)
    total = lax.dot_general(left, right, (((1,), (1,)), ((), ())), preferred_element_type=jnp.float32)
    total = total * factor
    lines = count // nm
    for m in range(nm):
        part[m, :, :2 * count] = total[m * lines:(m + 1) * lines]
    part_copies = []
    for k in range(1, nm):
        peer = lax.rem(column + k, nm)
        part_copies.append(pltpu.make_async_remote_copy(
            src_ref=part.at[peer], dst_ref=land.at[k - 1],
            send_sem=part_send_sem.at[k - 1], recv_sem=part_recv_sem.at[k - 1],
            device_id={"mat": peer}, device_id_type=MESH))
        part_copies[-1].start()
    result = part[column]
    for k in range(1, nm):
        part_copies[k - 1].wait_recv()
        result = result + land[k - 1]
    out_ref[...] = result

    for copy in list(copies.values()) + part_copies:
        copy.wait_send()


def local(traces, point_index, spectral_slot_number):
    shots, points, moments = traces.shape
    nf, nm = lax.axis_size("freq"), lax.axis_size("mat")
    assert spectral_slot_number.shape[0] == nf and points % LANES == 0
    assert moments & (moments - 1) == 0 and SUB * LANES % points == 0
    count, chunks = nf * shots, points // LANES
    lines = count // nm
    width = -(-2 * count // LANES) * LANES
    halves = 2
    factor = 4.0 / math.sqrt(points * nm)
    index = point_index.reshape(shots, chunks, LANES)
    any_space = pl.BlockSpec(memory_space=pltpu.HBM)
    result = pl.pallas_call(
        functools.partial(kernel, nf, nm, factor),
        out_shape=jax.ShapeDtypeStruct((lines, width), jnp.float32),
        in_specs=[any_space] * 3,
        out_specs=pl.BlockSpec(memory_space=pltpu.VMEM),
        scratch_shapes=[
            pltpu.SMEM(spectral_slot_number.shape, jnp.int32),
            pltpu.VMEM(index.shape, jnp.int32),
            pltpu.VMEM(traces.shape, jnp.bfloat16),
            pltpu.VMEM((2 * SUB * nf, moments), jnp.bfloat16),
            pltpu.VMEM((shots, nf, 2 * SUB, LANES), jnp.bfloat16),
            pltpu.VMEM((shots, nf, 2 * SUB, LANES), jnp.bfloat16),
            pltpu.VMEM((count * 2 * SUB, LANES), jnp.float32),
            pltpu.VMEM((nm, lines, width), jnp.float32),
            pltpu.VMEM((nm - 1, lines, width), jnp.float32),
            pltpu.SemaphoreType.DMA,
            pltpu.SemaphoreType.DMA,
            pltpu.SemaphoreType.DMA((shots, halves)),
            pltpu.SemaphoreType.DMA((shots, nf)),
            pltpu.SemaphoreType.DMA((shots, nf)),
            pltpu.SemaphoreType.DMA((nm - 1,)),
            pltpu.SemaphoreType.DMA((nm - 1,)),
        ],
        compiler_params=pltpu.CompilerParams(
            collective_id=0, has_side_effects=True, vmem_limit_bytes=32 * 1024 * 1024),
    )(traces, index, spectral_slot_number)
    return result[:, :2 * count].reshape(lines, 1, 2, count)


def solution(mesh):
    placed = (P(("groups", "freq"), "mat", None), P(("groups", "freq"), "mat", None), P("groups"))
    return jax.shard_map(
        local,
        mesh=mesh,
        in_specs=placed,
        out_specs=P(("groups", "mat"), "freq", None, None),
        check_vma=False,
    )
```

time: 47.2 us -> 16.1 us (0.34)
  local copies, waits for them, and re-layouts: 25.4 us -> 3.62 us
  Pallas kernels: 0 us -> 12.3 us
  starting transfers between devices: 6.33 us -> 0 us
  waiting for transfers between devices: 5.92 us -> 0 us
  blocking collectives: 4.94 us -> 0 us
  matrix products: 2.49 us -> 0 us
  other arithmetic: 1.74 us -> 0 us
    gather x1 -> x0, local copies, waits for them, and re-layouts: 24 us -> none  [reorder_rows(): return rows[order]]
    pallas_call x0 -> x1, Pallas kernels: none -> 12.3 us  [local(): pl.pallas_call(functools.partial(kernel, nf, nm, factor), out_shape=jax.S...]
    all_to_all x1 -> x0, starting transfers between devices: 6.33 us -> none  [local(): lax.all_to_all(spectra, 'freq', split_axis=0, concat_axis=2, tiled=True)]
    all_to_all x1 -> x0, waiting for transfers between devices: 5.92 us -> none  [local(): lax.all_to_all(spectra, 'freq', split_axis=0, concat_axis=2, tiled=True)]
    all_gather x1 -> x0, blocking collectives: 4.94 us -> none  [local(): panel = lax.all_gather(owned, 'mat', axis=3, tiled=True)]
    unnamed x2 -> x6, local copies, waits for them, and re-layouts: 0.01 us -> 2.94 us
    dot_general x2 -> x0, matrix products: 2.49 us -> none  [the longest x1 2.23 us: local(): jnp.einsum('jt,spt->jsp', fourier, ordered, preferred_element_type=jnp.fl...]
    another operation x3 -> x0, other arithmetic: 0.97 us -> none
  transfers between devices with their start and end apart: 1 -> 0, of which waited for: 1 -> 0; matrix products, arithmetic and copies ran while one was open for 0% -> 0% of each run, Pallas kernels for 0% -> 0%
where the time goes in v1:
time: 16.1 us; the launch traced here: 15.9 us
  Pallas kernels  12.3 us (76%)
  local copies, waits for them, and re-layouts  3.62 us (22%)
    pallas_call x1, Pallas kernels, local(): pl.pallas_call(functools.partial(kernel, nf, nm, factor), out_shape=jax.S...  12.3 us
    unnamed x6, local copies, waits for them, and re-layouts  2.94 us
    reshape x1, local copies, waits for them, and re-layouts, local(): return result[:, :2 * count].reshape(lines, 1, 2, count)  0.68 us

profile of v1, /device:TPU:0, one launch (start us, length us, event | category | flops | bytes accessed | tf_op | source)
XLA Modules:
  0.0 15.9 jit_solution(14300329741274755991)
XLA Ops:
  0.0 0.0 copy-start
  0.0 1.6 %copy-done = bf16[2,1024,512]{2,1,0:T(8,128)(2,1)S(1)} copy-done((bf16[2,1024,512]{2,1,0:T(8,128)(2,1)S(1)}, bf16[2,1024,512]{2,1,0:T(8,128)(2,1)}, u32[]{:S(2)}) %copy-start) | copy-done | bytes 2097176
  1.6 0.0 copy-start.1
  1.6 0.7 %copy-done.1 = s32[2,1,1024]{2,1,0:T(1,128)S(1)} copy-done((s32[2,1,1024]{2,1,0:T(1,128)S(1)}, s32[2,1,1024]{2,1,0:T(1,128)}, u32[]{:S(2)}) %copy-start.1) | copy-done | bytes 8216
  2.3 0.0 copy-start.2
  2.3 0.7 %copy-done.2 = s32[8]{0:T(128)S(1)} copy-done((s32[8]{0:T(128)S(1)}, s32[8]{0:T(128)}, u32[]{:S(2)}) %copy-start.2) | copy-done | bytes 56
  2.9 12.3 %shard_map.37 = f32[8,128]{1,0:T(8,128)S(1)} custom-call(bf16[2,1024,512]{2,1,0:T(8,128)(2,1)S(1)} %copy-done, s32[2,8,128]{2,1,0:T(8,128)S(1)} %bitcast.4, s32[8]{0:T(128)S(1)} %copy-done.2), custom_call_target="tpu_custom_call" | custom-call | tf_op jit(solution)/shard_map/pallas_call | solution.py:161
  15.2 0.7 %reshape.7 = f32[8,1,2,16]{3,2,0,1:T(2,128)} reshape(f32[8,32]{1,0:T(8,128)S(1)} %bitcast.3) | data formatting | bytes 2048 | tf_op jit(solution)/shard_map/reshape | solution.py:187
Async XLA Ops:
  0.0 1.6 %copy-start = (bf16[2,1024,512]{2,1,0:T(8,128)(2,1)S(1)}, bf16[2,1024,512]{2,1,0:T(8,128)(2,1)}, u32[]{:S(2)}) copy-start(bf16[2,1024,512]{2,1,0:T(8,128)(2,1)} %traces_hbm.1) | copy-start | bytes 6291460
  1.6 0.7 %copy-start.1 = (s32[2,1,1024]{2,1,0:T(1,128)S(1)}, s32[2,1,1024]{2,1,0:T(1,128)}, u32[]{:S(2)}) copy-start(s32[2,1,1024]{2,1,0:T(1,128)} %param.4) | copy-start | bytes 24580
  2.3 0.7 %copy-start.2 = (s32[8]{0:T(128)S(1)}, s32[8]{0:T(128)}, u32[]{:S(2)}) copy-start(s32[8]{0:T(128)} %slots_hbm.1) | copy-start | bytes 100

commit v2 on v1

--- a/solution.py
+++ b/solution.py
@@ -160,7 +160,7 @@
     any_space = pl.BlockSpec(memory_space=pltpu.HBM)
     result = pl.pallas_call(
         functools.partial(kernel, nf, nm, factor),
-        out_shape=jax.ShapeDtypeStruct((lines, width), jnp.float32),
+        out_shape=pltpu.VMEM((lines, width), jnp.float32),
         in_specs=[any_space] * 3,
         out_specs=pl.BlockSpec(memory_space=pltpu.VMEM),
         scratch_shapes=[
@@ -182,7 +182,7 @@
             pltpu.SemaphoreType.DMA((nm - 1,)),
         ],
         compiler_params=pltpu.CompilerParams(
-            collective_id=0, has_side_effects=True, vmem_limit_bytes=32 * 1024 * 1024),
+            collective_id=0, has_side_effects=True, vmem_limit_bytes=60 * 1024 * 1024),
     )(traces, index, spectral_slot_number)
     return result[:, :2 * count].reshape(lines, 1, 2, count)
 

time: 16.1 us -> 13.7 us (0.85)
  local copies, waits for them, and re-layouts: 3.62 us -> 0.68 us
  Pallas kernels: 12.3 us -> 12.9 us
    unnamed x6 -> x0, local copies, waits for them, and re-layouts: 2.94 us -> none
    pallas_call x1, Pallas kernels: 12.3 us -> 12.9 us  [local(): pl.pallas_call(functools.partial(kernel, nf, nm, factor), out_shape=pltpu...]
where the time goes in v2:
time: 13.7 us; the launch traced here: 13.6 us
  Pallas kernels  12.9 us (94%)
  local copies, waits for them, and re-layouts  0.68 us (5%)
    pallas_call x1, Pallas kernels, local(): pl.pallas_call(functools.partial(kernel, nf, nm, factor), out_shape=pltpu...  12.9 us
    reshape x1, local copies, waits for them, and re-layouts, local(): return result[:, :2 * count].reshape(lines, 1, 2, count)  0.68 us

profile of v2, /device:TPU:0, one launch (start us, length us, event | category | flops | bytes accessed | tf_op | source)
XLA Modules:
  0.0 13.6 jit_solution(14932103948935235451)
XLA Ops:
  0.0 12.9 %shard_map.37 = f32[8,128]{1,0:T(8,128)S(1)} custom-call(bf16[2,1024,512]{2,1,0:T(8,128)(2,1)} %traces_hbm.1, s32[2,8,128]{2,1,0:T(8,128)} %bitcast.4, s32[8]{0:T(128)} %slots_hbm.1), custom_call_target="tpu_custom_call" | custom-call | tf_op jit(solution)/shard_map/pallas_call | solution.py:161
  12.9 0.7 %reshape.7 = f32[8,1,2,16]{3,2,0,1:T(2,128)} reshape(f32[8,32]{1,0:T(8,128)S(1)} %bitcast.3) | data formatting | bytes 2048 | tf_op jit(solution)/shard_map/reshape | solution.py:187

commit v3 on v2

v3 whole, which is shorter than its diff:
```python
import functools
import math

import jax
import jax.numpy as jnp
from jax import lax
from jax.experimental import pallas as pl
from jax.experimental.pallas import tpu as pltpu
from jax.sharding import PartitionSpec as P

MESH = pl.DeviceIdType.MESH
LANES = 128
SUB = 8


def sine(x):
    y = x * x
    total = jnp.full_like(y, -1.0 / math.factorial(11))
    for order in (9, 7, 5, 3, 1):
        total = total * y + (-1.0) ** (order // 2) / math.factorial(order)
    return total * x


def cosine_of(turns, period):
    return sine((jnp.abs(turns - 0.5 * period) - 0.25 * period) * (2.0 * math.pi / period))


def kernel(nf, nm, factor, traces_hbm, index_hbm, slots_hbm, out_ref,
           slots, index, traces, table, send, recv, wide, whole,
           slot_sem, index_sem, trace_sem, send_sem, recv_sem):
    shots, points, moments = traces.shape
    chunks = points // LANES
    halves = trace_sem.shape[1]
    span = points // halves
    me, column = lax.axis_index("freq"), lax.axis_index("mat")
    peers = [(k, j) for k in list(range(1, nf)) + [0] for j in range(nm) if k or j]

    def device(k, j):
        return {"freq": lax.rem(me + k, nf), "mat": lax.rem(column + j, nm)}

    barrier = pltpu.get_barrier_semaphore()
    for k, j in peers:
        pl.semaphore_signal(barrier, inc=1, device_id=device(k, j), device_id_type=MESH)

    slot_copy = pltpu.make_async_copy(slots_hbm, slots, slot_sem)
    slot_copy.start()
    trace_copies = []
    for s in range(shots):
        trace_copies.append([])
        for h in range(halves):
            rows = pl.ds(h * span, span)
            copy = pltpu.make_async_copy(traces_hbm.at[s, rows], traces.at[s, rows], trace_sem.at[s, h])
            copy.start()
            trace_copies[s].append(copy)
        if s == 0:
            index_copy = pltpu.make_async_copy(index_hbm, index, index_sem)
            index_copy.start()

    moment = lax.broadcasted_iota(jnp.int32, (SUB, moments), 1)
    taper = 0.5 - 0.5 * cosine_of(moment.astype(jnp.float32) + 0.5, moments)
    weight = taper * (1.0 / math.sqrt(moments))
    row = lax.broadcasted_iota(jnp.int32, (SUB, moments), 0)
    slot_copy.wait()
    for base in range(0, nf, SUB):
        number = jnp.zeros((SUB, moments), jnp.int32)
        for k in range(base, min(base + SUB, nf)):
            number = jnp.where(row == k - base, slots[lax.rem(me + k, nf)], number)
        steps = (number * moment) & (moments - 1)
        quarter = (steps + moments // 4) & (moments - 1)
        pair = [cosine_of(m.astype(jnp.float32), moments) * weight for m in (steps, quarter)]
        for k in range(base, min(base + SUB, nf)):
            both = [jnp.broadcast_to(p[k - base:k - base + 1], (SUB, moments)) for p in pair]
            table[2 * SUB * k:2 * SUB * (k + 1), :] = jnp.concatenate(both, 0).astype(jnp.bfloat16)

    copies = {}

    def start(s, k):
        for j in range(nm):
            if k or j:
                copies[s, k, j] = pltpu.make_async_remote_copy(
                    src_ref=send.at[s, k], dst_ref=recv.at[j, s, k],
                    send_sem=send_sem.at[j, s, k], recv_sem=recv_sem.at[j, s, k],
                    device_id=device(k, j), device_id_type=MESH)
                copies[s, k, j].start()

    order = list(range(1, nf)) + [0]
    index_copy.wait()
    for s in range(shots):
        raw = []
        for h in range(halves):
            trace_copies[s][h].wait()
            raw.append(lax.dot_general(
                table[...], traces[s, h * span:(h + 1) * span, :], (((1,), (1,)), ((), ())),
                preferred_element_type=jnp.float32))
        raw = jnp.concatenate(raw, 1) if halves > 1 else raw[0]
        place = index[s]
        if chunks < SUB:
            place = jnp.concatenate([place] * (SUB // chunks), 0)
        low, high = place & (LANES - 1), place // LANES
        for k in order:
            both = []
            for c in range(2):
                first = (2 * k + c) * SUB
                got = None
                for j in range(chunks):
                    piece = raw[first:first + SUB, j * LANES:(j + 1) * LANES]
                    piece = jnp.take_along_axis(piece, low, axis=1)
                    got = piece if j == 0 else jnp.where(high == j, piece, got)
                both.append(got)
            send[s, k] = jnp.concatenate(both, 0).astype(jnp.bfloat16)
            if s:
                start(s, k)
        if s == 0:
            pl.semaphore_wait(barrier, len(peers))
            for k in order:
                start(s, k)

    count = nf * shots
    total = None
    for j in range(nm):
        for s in range(shots):
            for k in range(nf):
                if k or j:
                    copies[s, k, j].wait_recv()
                    block = recv[j, s, k]
                else:
                    block = send[s, k]
                source = lax.rem(me + nf - k, nf)
                first = pl.multiple_of((source * shots + s) * 2 * SUB, 2 * SUB)
                wide[j, pl.ds(first, 2 * SUB), :] = block.astype(jnp.float32)
        real, imag = [
            jnp.concatenate([wide[j, pl.ds(c * SUB + i, count, stride=2 * SUB), :] for i in range(chunks)], 1)
            for c in range(2)]
        left = jnp.concatenate([real, imag], 1).astype(jnp.bfloat16)
        right = jnp.concatenate(
            [jnp.concatenate([real, -imag], 1), jnp.concatenate([imag, real], 1)], 0).astype(jnp.bfloat16)
        term = lax.dot_general(left, right, (((1,), (1,)), ((), ())), preferred_element_type=jnp.float32)
        total = term if j == 0 else total + term
    lines = count // nm
    whole[:, :2 * count] = total * factor
    out_ref[:, :2 * count] = whole[pl.ds(pl.multiple_of(column * lines, lines), lines), :2 * count]

    for copy in copies.values():
        copy.wait_send()


def local(traces, point_index, spectral_slot_number):
    shots, points, moments = traces.shape
    nf, nm = lax.axis_size("freq"), lax.axis_size("mat")
    assert spectral_slot_number.shape[0] == nf and points % LANES == 0
    assert moments & (moments - 1) == 0 and SUB * LANES % points == 0
    count, chunks = nf * shots, points // LANES
    lines = count // nm
    width = -(-2 * count // LANES) * LANES
    halves = 2
    factor = 4.0 / math.sqrt(points * nm)
    index = point_index.reshape(shots, chunks, LANES)
    any_space = pl.BlockSpec(memory_space=pltpu.HBM)
    result = pl.pallas_call(
        functools.partial(kernel, nf, nm, factor),
        out_shape=pltpu.VMEM((lines, width), jnp.float32),
        in_specs=[any_space] * 3,
        out_specs=pl.BlockSpec(memory_space=pltpu.VMEM),
        scratch_shapes=[
            pltpu.SMEM(spectral_slot_number.shape, jnp.int32),
            pltpu.VMEM(index.shape, jnp.int32),
            pltpu.VMEM(traces.shape, jnp.bfloat16),
            pltpu.VMEM((2 * SUB * nf, moments), jnp.bfloat16),
            pltpu.VMEM((shots, nf, 2 * SUB, LANES), jnp.bfloat16),
            pltpu.VMEM((nm, shots, nf, 2 * SUB, LANES), jnp.bfloat16),
            pltpu.VMEM((nm, count * 2 * SUB, LANES), jnp.float32),
            pltpu.VMEM((count, width), jnp.float32),
            pltpu.SemaphoreType.DMA,
            pltpu.SemaphoreType.DMA,
            pltpu.SemaphoreType.DMA((shots, halves)),
            pltpu.SemaphoreType.DMA((nm, shots, nf)),
            pltpu.SemaphoreType.DMA((nm, shots, nf)),
        ],
        compiler_params=pltpu.CompilerParams(
            collective_id=0, has_side_effects=True, vmem_limit_bytes=60 * 1024 * 1024),
    )(traces, index, spectral_slot_number)
    return result[:, :2 * count].reshape(lines, 1, 2, count)


def solution(mesh):
    placed = (P(("groups", "freq"), "mat", None), P(("groups", "freq"), "mat", None), P("groups"))
    return jax.shard_map(
        local,
        mesh=mesh,
        in_specs=placed,
        out_specs=P(("groups", "mat"), "freq", None, None),
        check_vma=False,
    )
```

time: 13.7 us -> 12.3 us (0.90)
  Pallas kernels: 12.9 us -> 11.5 us
    pallas_call x1, Pallas kernels: 12.9 us -> 11.5 us  [local(): pl.pallas_call(functools.partial(kernel, nf, nm, factor), out_shape=pltpu...]
where the time goes in v3:
time: 12.3 us; the launch traced here: 12.2 us
  Pallas kernels  11.5 us (93%)
  local copies, waits for them, and re-layouts  0.68 us (6%)
    pallas_call x1, Pallas kernels, local(): pl.pallas_call(functools.partial(kernel, nf, nm, factor), out_shape=pltpu...  11.5 us
    reshape x1, local copies, waits for them, and re-layouts, local(): return result[:, :2 * count].reshape(lines, 1, 2, count)  0.68 us

profile of v3, /device:TPU:0, one launch (start us, length us, event | category | flops | bytes accessed | tf_op | source)
XLA Modules:
  0.0 12.2 jit_solution(15689933887668543232)
XLA Ops:
  0.0 11.5 %shard_map.37 = f32[8,128]{1,0:T(8,128)S(1)} custom-call(bf16[2,1024,512]{2,1,0:T(8,128)(2,1)} %traces_hbm.1, s32[2,8,128]{2,1,0:T(8,128)} %bitcast.4, s32[8]{0:T(128)} %slots_hbm.1), custom_call_target="tpu_custom_call" | custom-call | tf_op jit(solution)/shard_map/pallas_call | solution.py:159
  11.5 0.7 %reshape.7 = f32[8,1,2,16]{3,2,0,1:T(2,128)} reshape(f32[8,32]{1,0:T(8,128)S(1)} %bitcast.3) | data formatting | bytes 2048 | tf_op jit(solution)/shard_map/reshape | solution.py:182

commit v4 on v3

--- a/solution.py
+++ b/solution.py
@@ -38,10 +38,6 @@
     def device(k, j):
         return {"freq": lax.rem(me + k, nf), "mat": lax.rem(column + j, nm)}
 
-    barrier = pltpu.get_barrier_semaphore()
-    for k, j in peers:
-        pl.semaphore_signal(barrier, inc=1, device_id=device(k, j), device_id_type=MESH)
-
     slot_copy = pltpu.make_async_copy(slots_hbm, slots, slot_sem)
     slot_copy.start()
     trace_copies = []
@@ -55,6 +51,10 @@
         if s == 0:
             index_copy = pltpu.make_async_copy(index_hbm, index, index_sem)
             index_copy.start()
+
+    barrier = pltpu.get_barrier_semaphore()
+    for k, j in peers:
+        pl.semaphore_signal(barrier, inc=1, device_id=device(k, j), device_id_type=MESH)
 
     moment = lax.broadcasted_iota(jnp.int32, (SUB, moments), 1)
     taper = 0.5 - 0.5 * cosine_of(moment.astype(jnp.float32) + 0.5, moments)
@@ -74,14 +74,14 @@
 
     copies = {}
 
-    def start(s, k):
-        for j in range(nm):
+    def start(k):
+        for j in reversed(range(nm)):
             if k or j:
-                copies[s, k, j] = pltpu.make_async_remote_copy(
-                    src_ref=send.at[s, k], dst_ref=recv.at[j, s, k],
-                    send_sem=send_sem.at[j, s, k], recv_sem=recv_sem.at[j, s, k],
+                copies[k, j] = pltpu.make_async_remote_copy(
+                    src_ref=send.at[k], dst_ref=recv.at[j, k],
+                    send_sem=send_sem.at[j, k], recv_sem=recv_sem.at[j, k],
                     device_id=device(k, j), device_id_type=MESH)
-                copies[s, k, j].start()
+                copies[k, j].start()
 
     order = list(range(1, nf)) + [0]
     index_copy.wait()
@@ -107,13 +107,11 @@
                     piece = jnp.take_along_axis(piece, low, axis=1)
                     got = piece if j == 0 else jnp.where(high == j, piece, got)
                 both.append(got)
-            send[s, k] = jnp.concatenate(both, 0).astype(jnp.bfloat16)
-            if s:
-                start(s, k)
-        if s == 0:
+            send[k, s] = jnp.concatenate(both, 0).astype(jnp.bfloat16)
+        if s == shots - 1:
             pl.semaphore_wait(barrier, len(peers))
             for k in order:
-                start(s, k)
+                start(k)
 
     count = nf * shots
     total = None
@@ -121,10 +119,11 @@
         for s in range(shots):
             for k in range(nf):
                 if k or j:
-                    copies[s, k, j].wait_recv()
-                    block = recv[j, s, k]
+                    if s == 0:
+                        copies[k, j].wait_recv()
+                    block = recv[j, k, s]
                 else:
-                    block = send[s, k]
+                    block = send[k, s]
                 source = lax.rem(me + nf - k, nf)
                 first = pl.multiple_of((source * shots + s) * 2 * SUB, 2 * SUB)
                 wide[j, pl.ds(first, 2 * SUB), :] = block.astype(jnp.float32)
@@ -152,7 +151,7 @@
     count, chunks = nf * shots, points // LANES
     lines = count // nm
     width = -(-2 * count // LANES) * LANES
-    halves = 2
+    halves = 1
     factor = 4.0 / math.sqrt(points * nm)
     index = point_index.reshape(shots, chunks, LANES)
     any_space = pl.BlockSpec(memory_space=pltpu.HBM)
@@ -166,15 +165,15 @@
             pltpu.VMEM(index.shape, jnp.int32),
             pltpu.VMEM(traces.shape, jnp.bfloat16),
             pltpu.VMEM((2 * SUB * nf, moments), jnp.bfloat16),
-            pltpu.VMEM((shots, nf, 2 * SUB, LANES), jnp.bfloat16),
-            pltpu.VMEM((nm, shots, nf, 2 * SUB, LANES), jnp.bfloat16),
+            pltpu.VMEM((nf, shots, 2 * SUB, LANES), jnp.bfloat16),
+            pltpu.VMEM((nm, nf, shots, 2 * SUB, LANES), jnp.bfloat16),
             pltpu.VMEM((nm, count * 2 * SUB, LANES), jnp.float32),
             pltpu.VMEM((count, width), jnp.float32),
             pltpu.SemaphoreType.DMA,
             pltpu.SemaphoreType.DMA,
             pltpu.SemaphoreType.DMA((shots, halves)),
-            pltpu.SemaphoreType.DMA((nm, shots, nf)),
-            pltpu.SemaphoreType.DMA((nm, shots, nf)),
+            pltpu.SemaphoreType.DMA((nm, nf)),
+            pltpu.SemaphoreType.DMA((nm, nf)),
         ],
         compiler_params=pltpu.CompilerParams(
             collective_id=0, has_side_effects=True, vmem_limit_bytes=60 * 1024 * 1024),

time: 12.3 us -> 11.5 us (0.935)
  Pallas kernels: 11.5 us -> 10.7 us
    pallas_call x1, Pallas kernels: 11.5 us -> 10.7 us  [local(): pl.pallas_call(functools.partial(kernel, nf, nm, factor), out_shape=pltpu...]
where the time goes in v4:
time: 11.5 us; the launch traced here: 11.4 us
  Pallas kernels  10.7 us (93%)
  local copies, waits for them, and re-layouts  0.68 us (6%)
    pallas_call x1, Pallas kernels, local(): pl.pallas_call(functools.partial(kernel, nf, nm, factor), out_shape=pltpu...  10.7 us
    reshape x1, local copies, waits for them, and re-layouts, local(): return result[:, :2 * count].reshape(lines, 1, 2, count)  0.68 us

profile of v4, /device:TPU:0, one launch (start us, length us, event | category | flops | bytes accessed | tf_op | source)
XLA Modules:
  0.0 11.4 jit_solution(10143276864006925509)
XLA Ops:
  0.0 10.7 %shard_map.37 = f32[8,128]{1,0:T(8,128)S(1)} custom-call(bf16[2,1024,512]{2,1,0:T(8,128)(2,1)} %traces_hbm.1, s32[2,8,128]{2,1,0:T(8,128)} %bitcast.4, s32[8]{0:T(128)} %slots_hbm.1), custom_call_target="tpu_custom_call" | custom-call | tf_op jit(solution)/shard_map/pallas_call | solution.py:158
  10.7 0.7 %reshape.7 = f32[8,1,2,16]{3,2,0,1:T(2,128)} reshape(f32[8,32]{1,0:T(8,128)S(1)} %bitcast.3) | data formatting | bytes 2048 | tf_op jit(solution)/shard_map/reshape | solution.py:181
